TPU v7x, 32 devices: a whole 2x2x4 slice. The times are simulated.
32 devices in a mesh: groups: 2 (over y), rows: 4 (over z), sub: 4 (over x, core).
Axes of the slice: x: 2, y: 2, z: 4, core: 2. Of those that a mesh axis runs over, the one named last changes fastest.
Arguments:
- embeds: bfloat16 [32768, 256], P(('groups', 'rows')), parts along dimension 0, may hold values from -6 to 6
- start: float32 [64, 32768], P(None, ('groups', 'rows', 'sub')), parts along dimension 1, may hold values from -6 to 6
- pair_blocks: int32 [8, 4, 4, 2], P(('groups', 'rows'), 'sub'), parts along dimension 0, may hold values from 0 to 7, as said below
- pair_live: int32 [8, 4, 4], P(('groups', 'rows'), 'sub'), parts along dimension 0, may hold values from 0 to 1
Outputs:
- eigen_block: float32 [64, 32768], P(None, ('groups', 'rows', 'sub')), parts along dimension 1
There are 2 independent parts, one for each index of `groups`. A program takes and returns all parts, laid end to end along the dimension named above; each array names one. Nothing has to cross between parts.
Inputs may be any that keep to these rules, and one draw needn't show every extreme that they name: `pair_blocks`: every entry is a local block index. Where the destination t equals the rows index r, the partner block differs from the owner block. Every block of every rows index is the owner block of some slot with pair_live 1.
All inputs are finite; a program needn't handle non-finite values.
Results may differ from a plain program's by a relative error of at most 0.014.
The roundings to bfloat16 on the way count: a program that leaves them out, or rounds other values in their place, can miss the bound.
Values may be sent and summed in bfloat16 or wider, within the bound.
A program may use at most 128 MiB of HBM per device.

v0:
```python
import math

import jax
import jax.numpy as jnp
from jax import lax
from jax.sharding import PartitionSpec as P

BLOCK = 512


def unit_rows(embeds):
    values = embeds.astype(jnp.float32)
    scale = lax.rsqrt(jnp.mean(values * values, axis=1, keepdims=True) + 1e-05)
    return (values * scale * values.shape[1] ** (-0.5)).astype(jnp.bfloat16)


def build_group(operands):
    left_units, right_units, live_flags = operands
    sharpness = 2.0 * math.sqrt(left_units.shape[2])
    scores = jnp.einsum("sbf,scf->sbc", left_units, right_units, preferred_element_type=jnp.float32)
    weight = jnp.exp(sharpness * scores) * live_flags.astype(jnp.float32)[:, None, None]
    return weight.astype(jnp.bfloat16)


def build_tiles(left_units, right_units, live_flags):
    count = left_units.shape[0]
    group = math.gcd(count, 8)
    turns = count // group
    left_groups = left_units.reshape((turns, group) + left_units.shape[1:])
    right_groups = right_units.reshape((turns, group) + right_units.shape[1:])
    flag_groups = live_flags.reshape(turns, group)
    built = lax.map(build_group, (left_groups, right_groups, flag_groups))
    return built.reshape((count,) + built.shape[2:])


def fold_blocks(block_ids, values, count):
    selector = (block_ids[:, None] == jnp.arange(count, dtype=jnp.int32)[None, :]).astype(
        jnp.float32
    )
    return jnp.einsum("sj,s...->j...", selector, values, precision=lax.Precision.HIGHEST)


def per_device(embeds, start, pair_blocks, pair_live):
    slots = lax.axis_size("rows")
    shares = lax.axis_size("sub")
    width = start.shape[0]
    rows_dev = embeds.shape[0]
    blocks = rows_dev // BLOCK
    cols = rows_dev // shares
    total_rows = rows_dev * slots
    unit_blocks = unit_rows(embeds).reshape(blocks, BLOCK, embeds.shape[1])
    own_ids = pair_blocks[0, 0, :, 0]
    partner_ids = pair_blocks[0, 0, :, 1]
    live_flags = pair_live[0, 0]
    own_units = jnp.take(unit_blocks, own_ids, axis=0)
    served_ids = lax.all_to_all(partner_ids, "rows", split_axis=0, concat_axis=0, tiled=True)
    serve_units = jnp.take(unit_blocks, served_ids, axis=0)
    partner_units = lax.all_to_all(serve_units, "rows", split_axis=0, concat_axis=0, tiled=True)
    tiles = build_tiles(own_units, partner_units, live_flags)
    back_sums = lax.all_to_all(
        jnp.sum(tiles, axis=1, dtype=jnp.float32).astype(jnp.bfloat16),
        "rows",
        split_axis=0,
        concat_axis=0,
        tiled=True,
    ).astype(jnp.float32)
    own_sums = jnp.sum(tiles, axis=2, dtype=jnp.float32)
    degree_part = fold_blocks(own_ids, own_sums, blocks) + fold_blocks(
        served_ids, back_sums, blocks
    )
    degree = lax.psum(degree_part.reshape(rows_dev), "sub")
    inverse_root = lax.rsqrt(degree)
    first = lax.axis_index("sub") * cols
    inverse_slice = lax.dynamic_slice_in_dim(inverse_root, first, cols)
    scaled_full = lax.all_gather(
        (start * inverse_slice[None, :]).astype(jnp.bfloat16), "sub", axis=1, tiled=True
    )
    z_blocks = scaled_full.reshape(width, blocks, BLOCK).transpose(1, 0, 2)
    own_z = jnp.take(z_blocks, own_ids, axis=0)
    serve_z = jnp.take(z_blocks, served_ids, axis=0)
    partner_z = lax.all_to_all(serve_z, "rows", split_axis=0, concat_axis=0, tiled=True)
    outward = jnp.einsum("skb,sbc->skc", own_z, tiles, preferred_element_type=jnp.float32)
    guest = lax.all_to_all(
        outward.astype(jnp.bfloat16), "rows", split_axis=0, concat_axis=0, tiled=True
    ).astype(outward.dtype)
    owner_part = jnp.einsum("skc,sbc->skb", partner_z, tiles, preferred_element_type=jnp.float32)
    total = fold_blocks(own_ids, owner_part, blocks) + fold_blocks(served_ids, guest, blocks)
    products = lax.psum(
        total.transpose(1, 0, 2).reshape(width, rows_dev).astype(jnp.bfloat16), "sub"
    ).astype(jnp.float32)
    image = products * inverse_root[None, :]
    local_gram = jnp.dot(
        image, image.T, precision=lax.Precision.HIGHEST, preferred_element_type=jnp.float32
    )
    gram = lax.psum(local_gram, "rows")
    lower = jnp.linalg.cholesky(gram)
    basis = lax.linalg.triangular_solve(lower, image, left_side=True, lower=True)
    result = lax.dynamic_slice_in_dim(basis, first, cols, 1)
    return result * math.sqrt(total_rows)


def solution(mesh):
    placed = (
        P(("groups", "rows"), None),
        P(None, ("groups", "rows", "sub")),
        P(("groups", "rows"), "sub", None, None),
        P(("groups", "rows"), "sub", None),
    )
    return jax.shard_map(
        per_device,
        mesh=mesh,
        in_specs=placed,
        out_specs=P(None, ("groups", "rows", "sub")),
        check_vma=False,
    )
```

profile of v0, /device:TPU:0, one launch (start us, length us, event | category | flops | bytes accessed | tf_op | source)
XLA Modules:
  0.0 183.9 jit_solution(10169463567244517121)
XLA Ops:
  6.5 0.8 slice_bitcast_fusion.1
  7.3 0.7 copy.20
  8.0 6.3 %all-to-all-start = ((s32[4,1,1]{2,1,0:T(1,128)}), s32[4,1,1]{2,1,0:T(1,128)S(1)}, u32[]{:S(2)}, u32[]{:S(2)}) async-start(s32[4,1,1]{2,1,0:T(1,128)} %copy.20), calls=%async_computation | async-start | bytes 4096 | tf_op jit(solution)/shard_map/all_to_all | solution.py:56
  14.3 2.4 %fusion = f32[4096]{0:T(1024)S(1)} fusion(bf16[4096,256]{1,0:T(8,128)(2,1)} %param.8), kind=kLoop, calls=%fused_computation.6 | loop fusion | flops 3141632 | bytes 2113536 | tf_op jit(solution)/shard_map/reduce_sum | solution.py:13
  16.7 0.7 fusion.2
  17.4 2.3 %all-to-all-done = s32[4,1,1]{2,1,0:T(1,128)S(1)} async-done(((s32[4,1,1]{2,1,0:T(1,128)}), s32[4,1,1]{2,1,0:T(1,128)S(1)}, u32[]{:S(2)}, u32[]{:S(2)}) %all-to-all-start) | async-done | bytes 48 | tf_op jit(solution)/shard_map/all_to_all | solution.py:56
  20.6 1.2 broadcast_select_fusion
  21.8 4.4 %all-to-all-start.1 = ((bf16[4,512,256]{2,1,0:T(8,128)(2,1)}), bf16[4,512,256]{2,1,0:T(8,128)(2,1)}, u32[]{:S(2)}, u32[]{:S(2)}) async-start(bf16[4,512,256]{2,1,0:T(8,128)(2,1)} %broadcast_select_fusion), calls=%async_computation.1 | async-start | bytes 2097152 | tf_op jit(solution)/shard_map/all_to_all | solution.py:58
  26.8 23.9 %all-to-all-done.1 = bf16[4,512,256]{2,1,0:T(8,128)(2,1)} async-done(((bf16[4,512,256]{2,1,0:T(8,128)(2,1)}), bf16[4,512,256]{2,1,0:T(8,128)(2,1)}, u32[]{:S(2)}, u32[]{:S(2)}) %all-to-all-start.1) | async-done | bytes 1048608 | tf_op jit(solution)/shard_map/all_to_all | solution.py:58
  50.8 2.3 %convert_reduce_fusion = (f32[4,512]{1,0:T(4,128)S(1)}, bf16[4,512,512]{2,1,0:T(8,128)(2,1)S(1)}) fusion(f32[4]{0:T(128)S(1)} %convert_bitcast_fusion, bf16[4,512,256]{2,1,0:T(8,128)(2,1)} %all-to-all-done.1, bf16[4,512,256]{2,1,0:T(8,128)(2,1)S(1)} %gather_fusion, pred[4]{0:T(512)(128)(4,1)S(1)} %get-tuple-element.20), kind=kOutput, calls=%fused_computation.9 | convolution fusion | flops 542636032 | bytes 4202516 | tf_op jit(solution)/shard_map/while/body/eval_jaxpr/sbf,scf->sbc/dot_general | solution.py:20
  54.0 0.7 reduce.8
  55.2 3.2 %all-to-all-start.2 = ((bf16[4,2,256]{2,1,0:T(2,128)(2,1)}), bf16[4,2,256]{2,1,0:T(2,128)(2,1)S(1)}, u32[]{:S(2)}, u32[]{:S(2)}) async-start(bf16[4,2,256]{2,1,0:T(2,128)(2,1)} %reshape.113), calls=%async_computation.2 | async-start | bytes 8192 | tf_op jit(solution)/shard_map/all_to_all | solution.py:60
  58.7 5.3 %all-to-all-done.2 = bf16[4,2,256]{2,1,0:T(2,128)(2,1)S(1)} async-done(((bf16[4,2,256]{2,1,0:T(2,128)(2,1)}), bf16[4,2,256]{2,1,0:T(2,128)(2,1)S(1)}, u32[]{:S(2)}, u32[]{:S(2)}) %all-to-all-start.2) | async-done | bytes 4128 | tf_op jit(solution)/shard_map/all_to_all | solution.py:60
  64.3 10.1 %psum.21 = f32[4096]{0:T(1024)S(1)} all-reduce(f32[4096]{0:T(1024)S(1)} %bitcast.54), channel_id=1, replica_groups=mesh['groups'=2,'rows'=4,'sub'=4] {'sub'}, use_global_device_ids=true, to_apply=%region_3.5 | all-reduce | flops 4096 | bytes 32768 | tf_op jit(solution)/shard_map/psum | solution.py:71
  74.5 7.3 %all_gather.3 = bf16[64,4096]{1,0:T(8,128)(2,1)S(1)} all-gather(bf16[64,1024]{1,0:T(8,128)(2,1)S(1)} %multiply_convert_fusion.1), channel_id=1, replica_groups=mesh['groups'=2,'rows'=4,'sub'=4] {'sub'}, dimensions={1}, use_global_device_ids=true | all-gather | bytes 655360 | tf_op jit(solution)/shard_map/all_gather | solution.py:75
  82.4 0.8 broadcast_select_fusion.1
  83.2 3.4 %all-to-all-start.3 = ((bf16[4,64,512]{2,1,0:T(8,128)(2,1)}), bf16[4,64,512]{2,1,0:T(8,128)(2,1)S(1)}, u32[]{:S(2)}, u32[]{:S(2)}) async-start(bf16[4,64,512]{2,1,0:T(8,128)(2,1)} %broadcast_select_fusion.1), calls=%async_computation.3 | async-start | bytes 524288 | tf_op jit(solution)/shard_map/all_to_all | solution.py:81
  87.1 1.2 convolution_convert_fusion
  88.4 7.8 %all-to-all-done.3 = bf16[4,64,512]{2,1,0:T(8,128)(2,1)S(1)} async-done(((bf16[4,64,512]{2,1,0:T(8,128)(2,1)}), bf16[4,64,512]{2,1,0:T(8,128)(2,1)S(1)}, u32[]{:S(2)}, u32[]{:S(2)}) %all-to-all-start.3) | async-done | bytes 262176 | tf_op jit(solution)/shard_map/all_to_all | solution.py:81
  96.2 3.4 %all-to-all-start.4 = ((bf16[4,64,512]{2,1,0:T(8,128)(2,1)}), bf16[4,64,512]{2,1,0:T(8,128)(2,1)S(1)}, u32[]{:S(2)}, u32[]{:S(2)}) async-start(bf16[4,64,512]{2,1,0:T(8,128)(2,1)} %convolution_convert_fusion), calls=%async_computation.4 | async-start | bytes 524288 | tf_op jit(solution)/shard_map/all_to_all | solution.py:83
  99.7 0.7 fusion.34
  100.4 1.0 fusion.9
  101.4 6.3 %all-to-all-done.4 = bf16[4,64,512]{2,1,0:T(8,128)(2,1)S(1)} async-done(((bf16[4,64,512]{2,1,0:T(8,128)(2,1)}), bf16[4,64,512]{2,1,0:T(8,128)(2,1)S(1)}, u32[]{:S(2)}, u32[]{:S(2)}) %all-to-all-start.4) | async-done | bytes 262176 | tf_op jit(solution)/shard_map/all_to_all | solution.py:83
  108.1 1.0 copy.31
  109.2 31.6 %all-reduce.2.cloned.1.call-done = bf16[64,4096]{1,0:T(8,128)(2,1)} async-done(((bf16[64,4096]{1,0:T(8,128)(2,1)}), bf16[64,4096]{1,0:T(8,128)(2,1)}) %all-reduce.2.cloned.1.call-update) | async-done | bytes 524304 | tf_op jit(solution)/shard_map/psum | solution.py:88
  140.7 2.3 %fusion.7 = f32[64,64]{0,1:T(8,128)S(1)} fusion(bf16[64,4096]{1,0:T(8,128)(2,1)} %all-reduce.2.cloned.1.call-done, f32[4096]{0:T(1024)S(1)} %rsqrt.12), kind=kOutput, calls=%fused_computation.19 | convolution fusion | flops 201850880 | bytes 557056 | tf_op jit(solution)/shard_map/dot_general | solution.py:92
  143.0 19.0 %psum.23 = f32[64,64]{0,1:T(8,128)S(1)} all-reduce(f32[64,64]{0,1:T(8,128)S(1)} %fusion.7), channel_id=1, replica_groups=mesh['groups'=2,'rows'=4,'sub'=4] {'rows'}, use_global_device_ids=true, to_apply=%region_5.8 | all-reduce | flops 4096 | bytes 32768 | tf_op jit(solution)/shard_map/psum | solution.py:95
  162.1 5.8 %cholesky.16 = f32[64,64]{1,0:T(8,128)S(1)} custom-call(f32[64,64]{1,0:T(8,128)S(1)} %fusion.20), custom_call_target="Cholesky" | custom-call | tf_op jit(solution)/shard_map/jit(cholesky)/cholesky | solution.py:96
  168.6 0.7 fusion.18
  169.3 4.9 %custom-call.6 = f32[1,64,64]{1,2,0:T(8,128)S(1)} custom-call(f32[1,64,64]{2,1,0:T(8,128)S(1)} %fusion.18), custom_call_target="InvertDiagBlocksLowerTriangular" | custom-call | tf_op jit(solution)/shard_map/triangular_solve | solution.py:97
  174.2 2.1 %fusion.6 = f32[64,4096]{1,0:T(8,128)S(1)} fusion(bf16[64,4096]{1,0:T(8,128)(2,1)} %all-reduce.2.cloned.1.call-done, f32[4096]{0:T(1024)S(1)} %rsqrt.12, f32[1,64,64]{1,2,0:T(8,128)S(1)} %custom-call.6), kind=kOutput, calls=%fused_computation.18 | convolution fusion | flops 201850880 | bytes 1605632 | tf_op jit(solution)/shard_map/triangular_solve | solution.py:97
  176.3 0.7 dynamic-slice_multiply_fusion
  (38 shorter events, 5.8 us)
Async XLA Ops:
  8.0 11.8 %all-to-all-start = ((s32[4,1,1]{2,1,0:T(1,128)}), s32[4,1,1]{2,1,0:T(1,128)S(1)}, u32[]{:S(2)}, u32[]{:S(2)}) async-start(s32[4,1,1]{2,1,0:T(1,128)} %copy.20), calls=%async_computation | async-start | bytes 4096 | tf_op jit(solution)/shard_map/all_to_all | solution.py:56
  14.3 2.4 %copy-start = (bf16[4096,256]{1,0:T(8,128)(2,1)S(1)}, bf16[4096,256]{1,0:T(8,128)(2,1)}, u32[]{:S(2)}) copy-start(bf16[4096,256]{1,0:T(8,128)(2,1)} %param.8) | copy-start | bytes 6291460
  20.6 5.6 %copy-start.2 = (s32[1,1,4,2]{2,3,1,0:T(2,128)S(1)}, s32[1,1,4,2]{2,3,1,0:T(2,128)}, u32[]{:S(2)}) copy-start(s32[1,1,4,2]{2,3,1,0:T(2,128)} %param.10) | copy-start | bytes 100
  21.8 5.0 %copy-start.3 = (s32[1,1,4]{2,1,0:T(1,128)S(1)}, s32[1,1,4]{2,1,0:T(1,128)}, u32[]{:S(2)}) copy-start(s32[1,1,4]{2,1,0:T(1,128)} %param.11) | copy-start | bytes 52
  21.8 29.0 %all-to-all-start.1 = ((bf16[4,512,256]{2,1,0:T(8,128)(2,1)}), bf16[4,512,256]{2,1,0:T(8,128)(2,1)}, u32[]{:S(2)}, u32[]{:S(2)}) async-start(bf16[4,512,256]{2,1,0:T(8,128)(2,1)} %broadcast_select_fusion), calls=%async_computation.1 | async-start | bytes 2097152 | tf_op jit(solution)/shard_map/all_to_all | solution.py:58
  53.1 21.3 %copy-start.1 = (f32[64,1024]{1,0:T(8,128)S(1)}, f32[64,1024]{1,0:T(8,128)}, u32[]{:S(2)}) copy-start(f32[64,1024]{1,0:T(8,128)} %param.9) | copy-start | bytes 786436
  55.2 8.8 %all-to-all-start.2 = ((bf16[4,2,256]{2,1,0:T(2,128)(2,1)}), bf16[4,2,256]{2,1,0:T(2,128)(2,1)S(1)}, u32[]{:S(2)}, u32[]{:S(2)}) async-start(bf16[4,2,256]{2,1,0:T(2,128)(2,1)} %reshape.113), calls=%async_computation.2 | async-start | bytes 8192 | tf_op jit(solution)/shard_map/all_to_all | solution.py:60
  83.2 13.0 %all-to-all-start.3 = ((bf16[4,64,512]{2,1,0:T(8,128)(2,1)}), bf16[4,64,512]{2,1,0:T(8,128)(2,1)S(1)}, u32[]{:S(2)}, u32[]{:S(2)}) async-start(bf16[4,64,512]{2,1,0:T(8,128)(2,1)} %broadcast_select_fusion.1), calls=%async_computation.3 | async-start | bytes 524288 | tf_op jit(solution)/shard_map/all_to_all | solution.py:81
  96.2 11.5 %all-to-all-start.4 = ((bf16[4,64,512]{2,1,0:T(8,128)(2,1)}), bf16[4,64,512]{2,1,0:T(8,128)(2,1)S(1)}, u32[]{:S(2)}, u32[]{:S(2)}) async-start(bf16[4,64,512]{2,1,0:T(8,128)(2,1)} %convolution_convert_fusion), calls=%async_computation.4 | async-start | bytes 524288 | tf_op jit(solution)/shard_map/all_to_all | solution.py:83
  99.6 41.1 %all-reduce.2.cloned.1.call-start = ((), (), s32[]{:S(2)}) async-start(), calls=%async_computation.5 | async-start | bytes 1048576 | tf_op jit(solution)/shard_map/psum | solution.py:88
Sparse Core Ops, SparseCore 0:
  109.3 31.3 all-reduce.1
where the time goes:
time: 184 us
  waiting for transfers between devices  77.3 us (42%)
  blocking collectives  36.4 us (20%)
  starting transfers between devices  20.8 us (11%)
  other arithmetic  19.1 us (10%)
  between operations  13.7 us (7%)
  matrix products  10.6 us (6%)
  local copies, waits for them, and re-layouts  6.05 us (3%)
    psum x1, waiting for transfers between devices, per_device(): lax.psum(total.transpose(1, 0, 2).reshape(width, rows_dev).astype(jnp.bfl...  31.6 us
    all_to_all x1, waiting for transfers between devices, per_device(): lax.all_to_all(serve_units, 'rows', split_axis=0, concat_axis=0, tiled=True)  23.9 us
    psum x1, blocking collectives, per_device(): gram = lax.psum(local_gram, 'rows')  19 us
    psum x1, blocking collectives, per_device(): degree = lax.psum(degree_part.reshape(rows_dev), 'sub')  10.1 us
    all_to_all x1, waiting for transfers between devices, per_device(): lax.all_to_all(serve_z, 'rows', split_axis=0, concat_axis=0, tiled=True)  7.84 us
    all_gather x1, blocking collectives, per_device(): lax.all_gather((start * inverse_slice[None, :]).astype(jnp.bfloat16), 'su...  7.28 us
    another operation x3, other arithmetic, per_device(): lower = jnp.linalg.cholesky(gram)  6.52 us
    all_to_all x1, starting transfers between devices, per_device(): lax.all_to_all(partner_ids, 'rows', split_axis=0, concat_axis=0, tiled=True)  6.32 us
  transfers between devices with their start and end apart: 6, of which 6 were waited for; matrix products, arithmetic and copies ran while one was open for 4% of the time, Pallas kernels for 0%

commit v1 on v0

v1 whole, which is shorter than its diff:
```python
import functools
import math

import jax
import jax.numpy as jnp
from jax import lax
from jax.experimental import pallas as pl
from jax.experimental.pallas import tpu as pltpu
from jax.sharding import PartitionSpec as P

BLOCK = 512
MESH = pl.DeviceIdType.MESH
HIGH = lax.Precision.HIGHEST
F32 = jnp.float32
BF16 = jnp.bfloat16
IDS, UNITS, SUMS, SCALED, GUEST, GRAM_ROWS = range(6)
START, DEGREE, PRODUCTS, GRAM_SUB = range(4)


def each(count, body, first=0):
    if count <= 4:
        for i in range(first, count):
            body(i)
    else:

        def step(i, carry):
            body(i)
            return carry

        lax.fori_loop(first, count, step, 0)


def dot_t(left, right, **kw):
    return lax.dot_general(
        left, right, (((1,), (1,)), ((), ())), preferred_element_type=F32, **kw
    )


def subspace_kernel(
    slots, shares, own_ref, live_ref, ids_ref, embeds_ref, start_ref, image_ref, gram_ref,
    got_ids, served, units, sent_units, partner_units, tiles, col_sums, own_sums, got_sums,
    got_degree, degree_out, got_start, scaled, sent_scaled, partner_scaled, sent_guest, got_guest,
    owner_part, sent_products, got_products, gram_out, got_gram_sub, gram_part, got_gram_rows,
    row_send, row_recv, sub_send, sub_recv, local_sem,
):
    me_row = lax.axis_index("rows")
    me_sub = lax.axis_index("sub")
    blocks = units.shape[0]
    feat = units.shape[2]
    per_sub = blocks // shares
    other_row = lambda d: lax.rem(me_row + d, slots)
    other_sub = lambda d: lax.rem(me_sub + d, shares)

    def row_copy(kind, src, dst, at, arrives):
        return pltpu.make_async_remote_copy(
            src_ref=src, dst_ref=dst, send_sem=row_send.at[kind, at], recv_sem=row_recv.at[kind, arrives],
            device_id={"rows": at}, device_id_type=MESH,
        )

    def sub_copy(kind, src, dst, at, arrives):
        return pltpu.make_async_remote_copy(
            src_ref=src, dst_ref=dst, send_sem=sub_send.at[kind, at], recv_sem=sub_recv.at[kind, arrives],
            device_id={"sub": at}, device_id_type=MESH,
        )

    barrier = pltpu.get_barrier_semaphore()

    def greet_row(d):
        pl.semaphore_signal(barrier, inc=1, device_id={"rows": other_row(d)}, device_id_type=MESH)

    def greet_sub(d):
        pl.semaphore_signal(barrier, inc=1, device_id={"sub": other_sub(d)}, device_id_type=MESH)

    each(slots, greet_row, 1)
    each(shares, greet_sub, 1)
    pl.semaphore_wait(barrier, slots + shares - 2)

    each(slots, lambda d: row_copy(IDS, ids_ref.at[other_row(d)], got_ids.at[me_row], other_row(d), me_row).start(), 1)
    each(shares, lambda d: sub_copy(START, start_ref, got_start.at[me_sub], other_sub(d), me_sub).start(), 1)
    got_ids[me_row] = ids_ref[me_row]

    def normalise(j, carry):
        values = embeds_ref[pl.ds(pl.multiple_of(j * BLOCK, BLOCK), BLOCK), :].astype(F32)
        scale = lax.rsqrt(jnp.mean(values * values, axis=1, keepdims=True) + 1e-05)
        units[j] = (values * scale * feat ** (-0.5)).astype(BF16)
        return carry

    lax.fori_loop(0, blocks, normalise, 0)
    got_start[me_sub] = start_ref[...]

    each(slots, lambda d: row_copy(IDS, ids_ref.at[me_row], got_ids.at[other_row(d)], other_row(d), other_row(d)).wait_recv(), 1)
    to_scalar = pltpu.make_async_copy(got_ids, served, local_sem)
    to_scalar.start()
    to_scalar.wait()

    def serve_units(d):
        t = other_row(d)
        sent_units[t] = units[served[t, 0, 0]]
        row_copy(UNITS, sent_units.at[t], partner_units.at[me_row], t, me_row).start()

    each(slots, serve_units, 1)
    partner_units[me_row] = units[served[me_row, 0, 0]]

    sharpness = 2.0 * math.sqrt(feat)
    ones = jnp.ones((16, BLOCK), BF16)

    def build(d):
        t = other_row(d)
        if not (isinstance(d, int) and d == 0):
            row_copy(UNITS, sent_units.at[t], partner_units.at[t], t, t).wait_recv()
        live = live_ref[t].astype(F32)
        rows = 128

        def part(i, carry):
            at = pl.ds(pl.multiple_of(i * rows, rows), rows)
            scores = dot_t(units[own_ref[t], at, :], partner_units[t])
            tiles[t, at, :] = (jnp.exp(sharpness * scores) * live).astype(BF16)
            return carry

        lax.fori_loop(0, BLOCK // rows, part, 0)
        tile = tiles[t]
        col_sums[t] = jnp.dot(ones, tile, preferred_element_type=F32)[0:1]
        own_sums[t] = dot_t(ones, tile)[0:1]

    def build_and_send(d):
        t = other_row(d)
        build(d)
        row_copy(SUMS, col_sums.at[t], got_sums.at[me_row], t, me_row).start()

    build(0)
    got_sums[me_row] = col_sums[me_row]
    each(slots, build_and_send, 1)

    which = lax.broadcasted_iota(jnp.int32, (blocks, BLOCK), 0)
    degree_out[...] = jnp.zeros_like(degree_out)

    def fold_own(d):
        t = other_row(d)
        degree_out[...] += jnp.where(which == own_ref[t], own_sums[t], 0.0)

    def fold_served(d):
        t = other_row(d)
        if not (isinstance(d, int) and d == 0):
            row_copy(SUMS, col_sums.at[t], got_sums.at[t], t, t).wait_recv()
        degree_out[...] += jnp.where(which == served[t, 0, 0], got_sums[t], 0.0)

    fold_own(0)
    each(slots, fold_own, 1)
    fold_served(0)
    each(slots, fold_served, 1)
    each(shares, lambda d: sub_copy(DEGREE, degree_out, got_degree.at[me_sub], other_sub(d), me_sub).start(), 1)
    got_degree[me_sub] = degree_out[...]
    each(shares, lambda d: sub_copy(DEGREE, degree_out, got_degree.at[other_sub(d)], other_sub(d), other_sub(d)).wait_recv(), 1)
    inverse = lax.rsqrt(jnp.sum(got_degree[...], axis=0))

    each(shares, lambda d: sub_copy(START, start_ref, got_start.at[other_sub(d)], other_sub(d), other_sub(d)).wait_recv(), 1)
    for j in range(blocks):
        at = (j % per_sub) * BLOCK
        scaled[j] = (got_start[j // per_sub, :, at : at + BLOCK] * inverse[j : j + 1]).astype(BF16)

    def serve_scaled(d):
        t = other_row(d)
        sent_scaled[t] = scaled[served[t, 0, 0]]
        row_copy(SCALED, sent_scaled.at[t], partner_scaled.at[me_row], t, me_row).start()

    each(slots, serve_scaled, 1)
    partner_scaled[me_row] = scaled[served[me_row, 0, 0]]

    def outward(d):
        t = other_row(d)
        sent_guest[t] = jnp.dot(scaled[own_ref[t]], tiles[t], preferred_element_type=F32).astype(BF16)
        row_copy(GUEST, sent_guest.at[t], got_guest.at[me_row], t, me_row).start()

    each(slots, outward, 1)
    got_guest[me_row] = jnp.dot(scaled[own_ref[me_row]], tiles[me_row], preferred_element_type=F32).astype(BF16)
    owner_part[me_row] = dot_t(partner_scaled[me_row], tiles[me_row])

    def inward(d):
        t = other_row(d)
        row_copy(SCALED, sent_scaled.at[t], partner_scaled.at[t], t, t).wait_recv()
        owner_part[t] = dot_t(partner_scaled[t], tiles[t])

    each(slots, inward, 1)
    each(slots, lambda d: row_copy(GUEST, sent_guest.at[other_row(d)], got_guest.at[other_row(d)], other_row(d), other_row(d)).wait_recv(), 1)

    def total_of(j):
        total = jnp.zeros(owner_part.shape[1:], F32)

        def add(t, total):
            mine = jnp.where(own_ref[t] == j, 1.0, 0.0)
            guest = jnp.where(served[t, 0, 0] == j, 1.0, 0.0)
            return total + mine * owner_part[t] + guest * got_guest[t].astype(F32)

        if slots <= 4:
            for t in range(slots):
                total = add(t, total)
            return total
        return lax.fori_loop(0, slots, add, total)

    def share(d):
        to = other_sub(d)
        for b in range(per_sub):
            sent_products[to, :, b * BLOCK : (b + 1) * BLOCK] = total_of(to * per_sub + b).astype(BF16)
        sub_copy(PRODUCTS, sent_products.at[to], got_products.at[me_sub], to, me_sub).start()

    each(shares, share, 1)
    for b in range(per_sub):
        got_products[me_sub, :, b * BLOCK : (b + 1) * BLOCK] = total_of(me_sub * per_sub + b).astype(BF16)
    each(shares, lambda d: sub_copy(PRODUCTS, sent_products.at[me_sub], got_products.at[other_sub(d)], other_sub(d), other_sub(d)).wait_recv(), 1)

    for b in range(per_sub):
        cols = slice(b * BLOCK, (b + 1) * BLOCK)
        products = jnp.sum(got_products[:, :, cols].astype(F32), axis=0)
        mine = jnp.sum(jnp.where(which == me_sub * per_sub + b, inverse, 0.0), axis=0, keepdims=True)
        image_ref[:, cols] = products * mine
    image = image_ref[...]
    local = dot_t(image, image, precision=HIGH)
    gram_out[...] = local
    each(shares, lambda d: sub_copy(GRAM_SUB, gram_out, got_gram_sub.at[me_sub], other_sub(d), me_sub).start(), 1)
    got_gram_sub[me_sub] = local
    each(shares, lambda d: sub_copy(GRAM_SUB, gram_out, got_gram_sub.at[other_sub(d)], other_sub(d), other_sub(d)).wait_recv(), 1)
    part_sum = jnp.sum(got_gram_sub[...], axis=0)
    gram_part[...] = part_sum
    each(slots, lambda d: row_copy(GRAM_ROWS, gram_part, got_gram_rows.at[me_row], other_row(d), me_row).start(), 1)
    got_gram_rows[me_row] = part_sum
    each(slots, lambda d: row_copy(GRAM_ROWS, gram_part, got_gram_rows.at[other_row(d)], other_row(d), other_row(d)).wait_recv(), 1)
    gram_ref[...] = jnp.sum(got_gram_rows[...], axis=0)

    def sent_along_rows(d):
        t = other_row(d)
        row_copy(IDS, ids_ref.at[t], got_ids.at[me_row], t, me_row).wait_send()
        row_copy(UNITS, sent_units.at[t], partner_units.at[me_row], t, me_row).wait_send()
        row_copy(SUMS, col_sums.at[t], got_sums.at[me_row], t, me_row).wait_send()
        row_copy(SCALED, sent_scaled.at[t], partner_scaled.at[me_row], t, me_row).wait_send()
        row_copy(GUEST, sent_guest.at[t], got_guest.at[me_row], t, me_row).wait_send()
        row_copy(GRAM_ROWS, gram_part, got_gram_rows.at[me_row], t, me_row).wait_send()

    def sent_along_sub(d):
        to = other_sub(d)
        sub_copy(START, start_ref, got_start.at[me_sub], to, me_sub).wait_send()
        sub_copy(DEGREE, degree_out, got_degree.at[me_sub], to, me_sub).wait_send()
        sub_copy(PRODUCTS, sent_products.at[to], got_products.at[me_sub], to, me_sub).wait_send()
        sub_copy(GRAM_SUB, gram_out, got_gram_sub.at[me_sub], to, me_sub).wait_send()

    each(slots, sent_along_rows, 1)
    each(shares, sent_along_sub, 1)


def basis_kernel(size, gram_ref, image_ref, out_ref):
    width = gram_ref.shape[0]
    row = lax.broadcasted_iota(jnp.int32, (width, width), 0)
    col = lax.broadcasted_iota(jnp.int32, (width, width), 1)
    work = jnp.concatenate([gram_ref[...], jnp.where(row == col, 1.0, 0.0)], axis=1)
    below = lax.broadcasted_iota(jnp.int32, (width, 1), 0)
    for j in range(width):
        factor = jnp.where(below > j, work[:, j : j + 1] / work[j : j + 1, j : j + 1], 0.0)
        work = work - factor * work[j : j + 1, :]
    pivots = jnp.sum(jnp.where(row == col, work[:, :width], 0.0), axis=1, keepdims=True)
    lower_inverse = work[:, width:] * (lax.rsqrt(pivots) * size)
    out_ref[...] = jnp.dot(lower_inverse, image_ref[...], precision=HIGH, preferred_element_type=F32)


def per_device(embeds, start, pair_blocks, pair_live):
    slots = lax.axis_size("rows")
    shares = lax.axis_size("sub")
    width, cols = start.shape
    rows_dev, feat = embeds.shape
    blocks = rows_dev // BLOCK
    own_ids = pair_blocks[0, 0, :, 0]
    partner_ids = jnp.broadcast_to(pair_blocks[0, 0, :, 1][:, None, None], (slots, 1, 128))
    vmem = pl.BlockSpec(memory_space=pltpu.VMEM)
    smem = pl.BlockSpec(memory_space=pltpu.SMEM)
    dma = pltpu.SemaphoreType.DMA
    image, gram = pl.pallas_call(
        functools.partial(subspace_kernel, slots, shares),
        out_shape=[
            jax.ShapeDtypeStruct((width, cols), F32),
            jax.ShapeDtypeStruct((width, width), F32),
        ],
        in_specs=[smem, smem, vmem, vmem, vmem],
        out_specs=[vmem, vmem],
        scratch_shapes=[
            pltpu.VMEM((slots, 1, 128), jnp.int32),
            pltpu.SMEM((slots, 1, 128), jnp.int32),
            pltpu.VMEM((blocks, BLOCK, feat), BF16),
            pltpu.VMEM((slots, BLOCK, feat), BF16),
            pltpu.VMEM((slots, BLOCK, feat), BF16),
            pltpu.VMEM((slots, BLOCK, BLOCK), BF16),
            pltpu.VMEM((slots, 1, BLOCK), F32),
            pltpu.VMEM((slots, 1, BLOCK), F32),
            pltpu.VMEM((slots, 1, BLOCK), F32),
            pltpu.VMEM((shares, blocks, BLOCK), F32),
            pltpu.VMEM((blocks, BLOCK), F32),
            pltpu.VMEM((shares, width, cols), F32),
            pltpu.VMEM((blocks, width, BLOCK), BF16),
            pltpu.VMEM((slots, width, BLOCK), BF16),
            pltpu.VMEM((slots, width, BLOCK), BF16),
            pltpu.VMEM((slots, width, BLOCK), BF16),
            pltpu.VMEM((slots, width, BLOCK), BF16),
            pltpu.VMEM((slots, width, BLOCK), F32),
            pltpu.VMEM((shares, width, cols), BF16),
            pltpu.VMEM((shares, width, cols), BF16),
            pltpu.VMEM((width, width), F32),
            pltpu.VMEM((shares, width, width), F32),
            pltpu.VMEM((width, width), F32),
            pltpu.VMEM((slots, width, width), F32),
            dma((6, slots)),
            dma((6, slots)),
            dma((4, shares)),
            dma((4, shares)),
            dma(()),
        ],
        compiler_params=pltpu.CompilerParams(
            collective_id=0, has_side_effects=True, vmem_limit_bytes=60 * 2**20
        ),
        name="subspace",
    )(own_ids, pair_live[0, 0], partner_ids, embeds, start)
    return pl.pallas_call(
        functools.partial(basis_kernel, math.sqrt(rows_dev * slots)),
        out_shape=jax.ShapeDtypeStruct((width, cols), F32),
        in_specs=[vmem, vmem],
        out_specs=vmem,
        compiler_params=pltpu.CompilerParams(vmem_limit_bytes=32 * 2**20),
        name="basis",
    )(gram, image)


def solution(mesh):
    placed = (
        P(("groups", "rows"), None),
        P(None, ("groups", "rows", "sub")),
        P(("groups", "rows"), "sub", None, None),
        P(("groups", "rows"), "sub", None),
    )
    return jax.shard_map(
        per_device,
        mesh=mesh,
        in_specs=placed,
        out_specs=P(None, ("groups", "rows", "sub")),
        check_vma=False,
    )
```

time: 184 us -> 80.7 us (0.44)
  waiting for transfers between devices: 77.3 us -> 0 us
  Pallas kernels: 0 us -> 76.8 us
  blocking collectives: 36.4 us -> 0 us
  starting transfers between devices: 20.8 us -> 0 us
  other arithmetic: 19.1 us -> 0 us
  between operations: 13.7 us -> 0.02 us
  matrix products: 10.6 us -> 0 us
  local copies, waits for them, and re-layouts: 6.05 us -> 3.63 us
    pallas_call x0 -> x2, Pallas kernels: none -> 76.8 us  [the longest x1 70.3 us: per_device(): pl.pallas_call(functools.partial(subspace_kernel, slots, shares), out_sha...]
    all_to_all x5 -> x0, waiting for transfers between devices: 45.7 us -> none  [the longest x1 23.9 us: per_device(): lax.all_to_all(serve_units, 'rows', split_axis=0, concat_axis=0, tiled=True)]
    psum x1 -> x0, waiting for transfers between devices: 31.6 us -> none  [per_device(): lax.psum(total.transpose(1, 0, 2).reshape(width, rows_dev).astype(jnp.bfl...]
    psum x2 -> x0, blocking collectives: 29.1 us -> none  [the longest x1 19 us: per_device(): gram = lax.psum(local_gram, 'rows')]
    all_to_all x5 -> x0, starting transfers between devices: 20.7 us -> none  [the longest x1 6.32 us: per_device(): lax.all_to_all(partner_ids, 'rows', split_axis=0, concat_axis=0, tiled=True)]
    another operation x5 -> x0, other arithmetic: 12.1 us -> none  [the longest x3 6.52 us: per_device(): lower = jnp.linalg.cholesky(gram)]
    dot_general x8 -> x0, matrix products: 8.55 us -> none  [the longest x1 2.34 us: build_group(): jnp.einsum('sbf,scf->sbc', left_units, right_units, preferred_element_typ...]
    all_gather x1 -> x0, blocking collectives: 7.28 us -> none  [per_device(): lax.all_gather((start * inverse_slice[None, :]).astype(jnp.bfloat16), 'su...]
  transfers between devices with their start and end apart: 6 -> 0, of which waited for: 6 -> 0; matrix products, arithmetic and copies ran while one was open for 4% -> 0% of each run, Pallas kernels for 0% -> 0%
where the time goes in v1:
time: 80.7 us; the launch traced here: 80.4 us
  Pallas kernels  76.8 us (95%)
  local copies, waits for them, and re-layouts  3.63 us (4%)
    pallas_call x1, Pallas kernels, per_device(): pl.pallas_call(functools.partial(subspace_kernel, slots, shares), out_sha...  70.3 us
    pallas_call x1, Pallas kernels, per_device(): pl.pallas_call(functools.partial(basis_kernel, math.sqrt(rows_dev * slots...  6.52 us
    broadcast_in_dim x2, local copies, waits for them, and re-layouts, per_device(): jnp.broadcast_to(pair_blocks[0, 0, :, 1][:, None, None], (slots, 1, 128))  1.93 us
    unnamed x4, local copies, waits for them, and re-layouts  1.7 us

profile of v1, /device:TPU:0, one launch (start us, length us, event | category | flops | bytes accessed | tf_op | source)
XLA Modules:
  0.0 80.4 jit_solution(13191514523367232364)
XLA Ops:
  0.0 1.3 %slice_bitcast_fusion = (s32[4]{0:T(128)S(1)}, s32[4]{0:T(128)}) fusion(s32[1,1,4,2]{2,3,1,0:T(2,128)} %param.6), kind=kLoop, calls=%fused_computation | loop fusion | bytes 64 | tf_op jit(solution)/shard_map/broadcast_in_dim | solution.py:270
  1.3 0.6 broadcast_in_dim.8.ids_ref
  1.9 70.3 %subspace.1 = (f32[64,1024]{1,0:T(8,128)}, f32[64,64]{1,0:T(8,128)}) custom-call(s32[4]{0:T(128)} %get-tuple-element.10.own_ref, s32[4]{0:T(128)} %bitcast.5, s32[4,1,128]{2,1,0:T(1,128)} %broadcast_in_dim.8.ids_ref, bf16[4096,256]{1,0:T(8,128)(2,1)} %embeds_ref.1, f32[64,1024]{1,0:T(8,128)} %start_ref.1), custom_call_target="tpu_custom_call" | custom-call | tf_op jit(solution)/shard_map/subspace/pallas_call | solution.py:274
  72.2 0.0 copy-start
  72.2 0.9 %copy-done = f32[64,1024]{1,0:T(8,128)S(1)} copy-done((f32[64,1024]{1,0:T(8,128)S(1)}, f32[64,1024]{1,0:T(8,128)}, u32[]{:S(2)}) %copy-start) | copy-done | bytes 262168
  73.2 0.0 copy-start.1
  73.2 0.8 copy-done.1
  73.9 6.5 %basis.1 = f32[64,1024]{1,0:T(8,128)} custom-call(f32[64,64]{1,0:T(8,128)S(1)} %copy-done.1, f32[64,1024]{1,0:T(8,128)S(1)} %copy-done), custom_call_target="tpu_custom_call" | custom-call | tf_op jit(solution)/shard_map/basis/pallas_call | solution.py:318
Async XLA Ops:
  72.2 1.0 %copy-start = (f32[64,1024]{1,0:T(8,128)S(1)}, f32[64,1024]{1,0:T(8,128)}, u32[]{:S(2)}) copy-start(f32[64,1024]{1,0:T(8,128)} %get-tuple-element.8.image_ref) | copy-start | bytes 786436
  73.2 0.8 copy-start.1

commit v2 on v1

v2 whole, which is shorter than its diff:
```python
import functools
import math

import jax
import jax.numpy as jnp
from jax import lax
from jax.experimental import pallas as pl
from jax.experimental.pallas import tpu as pltpu
from jax.sharding import PartitionSpec as P

BLOCK = 512
HALVES = 2
MESH = pl.DeviceIdType.MESH
HIGH = lax.Precision.HIGHEST
F32 = jnp.float32
BF16 = jnp.bfloat16
META, SUMS, SCALED, PRODUCT, GRAM_ROWS = range(5)
START, DEGREE, PRODUCTS, GRAM_SUB = range(4)


def each(count, body, first=0):
    if count <= 4:
        for i in range(first, count):
            body(i)
    else:

        def step(i, carry):
            body(i)
            return carry

        lax.fori_loop(first, count, step, 0)


def dot_t(left, right, **kw):
    return lax.dot_general(
        left, right, (((1,), (1,)), ((), ())), preferred_element_type=F32, **kw
    )


def subspace_kernel(
    slots, shares, pairs_ref, live_ref, embeds_hbm, start_hbm, image_ref, gram_ref,
    embeds, sent_meta, got_meta, served, units, sent_units, got_units, tiles, col_sums, own_sums, got_sums,
    got_degree, degree_out, got_start, scaled, sent_scaled, got_scaled, sent_product, got_product,
    local_part, sent_products, got_products, gram_out, got_gram_sub, gram_part, got_gram_rows,
    row_send, row_recv, unit_send, unit_recv, sub_send, sub_recv, local_sem,
):
    me_row = lax.axis_index("rows")
    me_sub = lax.axis_index("sub")
    blocks, _, feat = units.shape
    width = scaled.shape[1]
    per_sub = blocks // shares
    half = BLOCK // HALVES
    other_row = lambda d: lax.rem(me_row + d, slots)
    other_sub = lambda d: lax.rem(me_sub + d, shares)
    own = lambda t: pairs_ref[0, 0, t, 0]
    partner = lambda r: served[r, 0, 0]

    load_embeds = pltpu.make_async_copy(embeds_hbm, embeds, local_sem.at[0])
    load_embeds.start()
    load_start = pltpu.make_async_copy(start_hbm, got_start.at[me_sub], local_sem.at[1])
    load_start.start()

    def row_copy(kind, src, dst, at, arrives):
        return pltpu.make_async_remote_copy(
            src_ref=src, dst_ref=dst, send_sem=row_send.at[kind, at], recv_sem=row_recv.at[kind, arrives],
            device_id={"rows": at}, device_id_type=MESH,
        )

    def unit_copy(h, at, arrives):
        part = pl.ds(h * half, half)
        return pltpu.make_async_remote_copy(
            src_ref=sent_units.at[at, part], dst_ref=got_units.at[arrives, part],
            send_sem=unit_send.at[h, at], recv_sem=unit_recv.at[h, arrives],
            device_id={"rows": at}, device_id_type=MESH,
        )

    def sub_copy(kind, src, dst, at, arrives):
        return pltpu.make_async_remote_copy(
            src_ref=src, dst_ref=dst, send_sem=sub_send.at[kind, at], recv_sem=sub_recv.at[kind, arrives],
            device_id={"sub": at}, device_id_type=MESH,
        )

    barrier = pltpu.get_barrier_semaphore()

    def greet_row(d):
        pl.semaphore_signal(barrier, inc=1, device_id={"rows": other_row(d)}, device_id_type=MESH)

    def greet_sub(d):
        pl.semaphore_signal(barrier, inc=1, device_id={"sub": other_sub(d)}, device_id_type=MESH)

    each(slots, greet_row, 1)
    each(shares, greet_sub, 1)

    lane = lax.broadcasted_iota(jnp.int32, (1, 128), 1)

    def put_meta(d):
        t = other_row(d)
        sent_meta[t] = jnp.where(lane == 0, pairs_ref[0, 0, t, 1], live_ref[0, 0, t])

    each(slots, put_meta)

    def unit_rows(values):
        values = values.astype(F32)
        scale = lax.rsqrt(jnp.mean(values * values, axis=1, keepdims=True) + 1e-05)
        return (values * scale * feat ** (-0.5)).astype(BF16)

    load_embeds.wait()

    def fill(h, d):
        t = other_row(d)
        part = pl.ds(h * half, half)
        sent_units[t, part, :] = unit_rows(embeds[own(t), part, :])

    each(slots, lambda d: fill(0, d), 1)
    pl.semaphore_wait(barrier, slots + shares - 2)
    for h in range(HALVES):
        if h:
            each(slots, lambda d: fill(h, d), 1)
        each(slots, lambda d: unit_copy(h, other_row(d), me_row).start(), 1)
        if h == 0:
            each(slots, lambda d: row_copy(META, sent_meta.at[other_row(d)], got_meta.at[me_row], other_row(d), me_row).start(), 1)
    load_start.wait()
    each(shares, lambda d: sub_copy(START, got_start.at[me_sub], got_start.at[me_sub], other_sub(d), me_sub).start(), 1)
    got_meta[me_row] = sent_meta[me_row]

    def normalise(j, carry):
        units[j] = unit_rows(embeds[j])
        return carry

    lax.fori_loop(0, blocks, normalise, 0)
    got_units[me_row] = units[own(me_row)]

    each(slots, lambda d: row_copy(META, sent_meta.at[me_row], got_meta.at[other_row(d)], other_row(d), other_row(d)).wait_recv(), 1)
    to_scalar = pltpu.make_async_copy(got_meta, served, local_sem.at[2])
    to_scalar.start()
    to_scalar.wait()

    sharpness = 2.0 * math.sqrt(feat)
    ones = jnp.ones((16, BLOCK), BF16)
    rows = 128

    def build(h, d):
        r = other_row(d)
        remote = not (isinstance(d, int) and d == 0)
        if remote:
            unit_copy(h, me_row, r).wait_recv()
        live = served[r, 0, 1].astype(F32)

        def part(i, sums):
            at = pl.ds(pl.multiple_of(h * half + i * rows, rows), rows)
            scores = dot_t(got_units[r, at, :], units[partner(r)])
            tile = (jnp.exp(sharpness * scores) * live).astype(BF16)
            tiles[r, at, :] = tile
            return sums + jnp.sum(tile.astype(F32).reshape(rows // 8, 8, BLOCK), axis=0)

        sums = lax.fori_loop(0, half // rows, part, jnp.zeros((8, BLOCK), F32))
        sums = jnp.sum(sums, axis=0, keepdims=True)
        col_sums[r] = sums if h == 0 else col_sums[r] + sums
        if h == HALVES - 1:
            own_sums[r] = dot_t(ones, tiles[r])[0:1]
            if remote:
                row_copy(SUMS, own_sums.at[r], got_sums.at[me_row], r, me_row).start()

    for h in range(HALVES):
        build(h, 0)
    got_sums[me_row] = own_sums[me_row]
    for h in range(HALVES):
        each(slots, lambda d: build(h, d), 1)

    which = lax.broadcasted_iota(jnp.int32, (blocks, BLOCK), 0)
    degree_out[...] = jnp.zeros_like(degree_out)

    def fold_partner(d):
        r = other_row(d)
        degree_out[...] += jnp.where(which == partner(r), col_sums[r], 0.0)

    def fold_own(d):
        t = other_row(d)
        if not (isinstance(d, int) and d == 0):
            row_copy(SUMS, own_sums.at[t], got_sums.at[t], t, t).wait_recv()
        degree_out[...] += jnp.where(which == own(t), got_sums[t], 0.0)

    each(slots, fold_partner)
    fold_own(0)
    each(slots, fold_own, 1)
    each(shares, lambda d: sub_copy(DEGREE, degree_out, got_degree.at[me_sub], other_sub(d), me_sub).start(), 1)
    got_degree[me_sub] = degree_out[...]
    each(shares, lambda d: sub_copy(START, got_start.at[me_sub], got_start.at[other_sub(d)], other_sub(d), other_sub(d)).wait_recv(), 1)
    each(shares, lambda d: sub_copy(DEGREE, degree_out, got_degree.at[other_sub(d)], other_sub(d), other_sub(d)).wait_recv(), 1)
    inverse = lax.rsqrt(jnp.sum(got_degree[...], axis=0))

    for j in range(blocks):
        at = (j % per_sub) * BLOCK
        scaled[j] = (got_start[j // per_sub, :, at : at + BLOCK] * inverse[j : j + 1]).astype(BF16)

    def serve_scaled(d):
        t = other_row(d)
        sent_scaled[t] = scaled[own(t)]
        row_copy(SCALED, sent_scaled.at[t], got_scaled.at[me_row], t, me_row).start()

    each(slots, serve_scaled, 1)
    got_scaled[me_row] = scaled[own(me_row)]

    def back(d):
        r = other_row(d)
        sent_product[r] = dot_t(scaled[partner(r)], tiles[r]).astype(BF16)
        row_copy(PRODUCT, sent_product.at[r], got_product.at[me_row], r, me_row).start()

    each(slots, back, 1)
    got_product[me_row] = dot_t(scaled[partner(me_row)], tiles[me_row]).astype(BF16)

    def stay(d):
        r = other_row(d)
        if not (isinstance(d, int) and d == 0):
            row_copy(SCALED, sent_scaled.at[r], got_scaled.at[r], r, r).wait_recv()
        local_part[r] = jnp.dot(got_scaled[r], tiles[r], preferred_element_type=F32)

    stay(0)
    each(slots, stay, 1)
    each(slots, lambda d: row_copy(PRODUCT, sent_product.at[other_row(d)], got_product.at[other_row(d)], other_row(d), other_row(d)).wait_recv(), 1)

    def total_of(j):
        total = jnp.zeros(local_part.shape[1:], F32)

        def add(t, total):
            there = jnp.where(own(t) == j, 1.0, 0.0)
            here = jnp.where(partner(t) == j, 1.0, 0.0)
            return total + here * local_part[t] + there * got_product[t].astype(F32)

        if slots <= 4:
            for t in range(slots):
                total = add(t, total)
            return total
        return lax.fori_loop(0, slots, add, total)

    def share(d):
        to = other_sub(d)
        for b in range(per_sub):
            sent_products[to, :, b * BLOCK : (b + 1) * BLOCK] = total_of(to * per_sub + b).astype(BF16)
        sub_copy(PRODUCTS, sent_products.at[to], got_products.at[me_sub], to, me_sub).start()

    each(shares, share, 1)
    for b in range(per_sub):
        got_products[me_sub, :, b * BLOCK : (b + 1) * BLOCK] = total_of(me_sub * per_sub + b).astype(BF16)
    each(shares, lambda d: sub_copy(PRODUCTS, sent_products.at[me_sub], got_products.at[other_sub(d)], other_sub(d), other_sub(d)).wait_recv(), 1)

    for b in range(per_sub):
        cols = slice(b * BLOCK, (b + 1) * BLOCK)
        products = jnp.sum(got_products[:, :, cols].astype(F32), axis=0)
        mine = jnp.sum(jnp.where(which == me_sub * per_sub + b, inverse, 0.0), axis=0, keepdims=True)
        image_ref[:, cols] = products * mine
    image = image_ref[...]
    local = dot_t(image, image, precision=HIGH)
    local = jnp.concatenate([local[: width // 2], local[width // 2 :]], axis=1)
    gram_out[...] = local
    each(shares, lambda d: sub_copy(GRAM_SUB, gram_out, got_gram_sub.at[me_sub], other_sub(d), me_sub).start(), 1)
    got_gram_sub[me_sub] = local
    each(shares, lambda d: sub_copy(GRAM_SUB, gram_out, got_gram_sub.at[other_sub(d)], other_sub(d), other_sub(d)).wait_recv(), 1)
    part_sum = jnp.sum(got_gram_sub[...], axis=0)
    gram_part[...] = part_sum
    each(slots, lambda d: row_copy(GRAM_ROWS, gram_part, got_gram_rows.at[me_row], other_row(d), me_row).start(), 1)
    got_gram_rows[me_row] = part_sum
    each(slots, lambda d: row_copy(GRAM_ROWS, gram_part, got_gram_rows.at[other_row(d)], other_row(d), other_row(d)).wait_recv(), 1)
    gram_ref[...] = jnp.sum(got_gram_rows[...], axis=0)

    def sent_along_rows(d):
        t = other_row(d)
        row_copy(META, sent_meta.at[t], got_meta.at[me_row], t, me_row).wait_send()
        for h in range(HALVES):
            unit_copy(h, t, me_row).wait_send()
        row_copy(SUMS, own_sums.at[t], got_sums.at[me_row], t, me_row).wait_send()
        row_copy(SCALED, sent_scaled.at[t], got_scaled.at[me_row], t, me_row).wait_send()
        row_copy(PRODUCT, sent_product.at[t], got_product.at[me_row], t, me_row).wait_send()
        row_copy(GRAM_ROWS, gram_part, got_gram_rows.at[me_row], t, me_row).wait_send()

    def sent_along_sub(d):
        to = other_sub(d)
        sub_copy(START, got_start.at[me_sub], got_start.at[me_sub], to, me_sub).wait_send()
        sub_copy(DEGREE, degree_out, got_degree.at[me_sub], to, me_sub).wait_send()
        sub_copy(PRODUCTS, sent_products.at[to], got_products.at[me_sub], to, me_sub).wait_send()
        sub_copy(GRAM_SUB, gram_out, got_gram_sub.at[me_sub], to, me_sub).wait_send()

    each(slots, sent_along_rows, 1)
    each(shares, sent_along_sub, 1)


def basis_kernel(size, gram_ref, image_ref, out_ref):
    width = gram_ref.shape[0] * 2
    packed = gram_ref[...]
    gram = jnp.concatenate([packed[:, :width], packed[:, width:]], axis=0)
    row = lax.broadcasted_iota(jnp.int32, (width, width), 0)
    col = lax.broadcasted_iota(jnp.int32, (width, width), 1)
    work = jnp.concatenate([gram, jnp.where(row == col, 1.0, 0.0)], axis=1)
    below = lax.broadcasted_iota(jnp.int32, (width, 1), 0)
    for j in range(width):
        factor = jnp.where(below > j, work[:, j : j + 1] / work[j : j + 1, j : j + 1], 0.0)
        work = work - factor * work[j : j + 1, :]
    pivots = jnp.sum(jnp.where(row == col, work[:, :width], 0.0), axis=1, keepdims=True)
    lower_inverse = work[:, width:] * (lax.rsqrt(pivots) * size)
    out_ref[...] = jnp.dot(lower_inverse, image_ref[...], precision=HIGH, preferred_element_type=F32)


def per_device(embeds, start, pair_blocks, pair_live):
    slots = lax.axis_size("rows")
    shares = lax.axis_size("sub")
    width, cols = start.shape
    rows_dev, feat = embeds.shape
    blocks = rows_dev // BLOCK
    vmem = pl.BlockSpec(memory_space=pltpu.VMEM)
    smem = pl.BlockSpec(memory_space=pltpu.SMEM)
    dma = pltpu.SemaphoreType.DMA
    image, gram = pl.pallas_call(
        functools.partial(subspace_kernel, slots, shares),
        out_shape=[
            jax.ShapeDtypeStruct((width, cols), F32),
            jax.ShapeDtypeStruct((width // 2, 2 * width), F32),
        ],
        in_specs=[smem, smem, pl.BlockSpec(memory_space=pl.ANY), pl.BlockSpec(memory_space=pl.ANY)],
        out_specs=[vmem, vmem],
        scratch_shapes=[
            pltpu.VMEM((blocks, BLOCK, feat), BF16),
            pltpu.VMEM((slots, 1, 128), jnp.int32),
            pltpu.VMEM((slots, 1, 128), jnp.int32),
            pltpu.SMEM((slots, 1, 128), jnp.int32),
            pltpu.VMEM((blocks, BLOCK, feat), BF16),
            pltpu.VMEM((slots, BLOCK, feat), BF16),
            pltpu.VMEM((slots, BLOCK, feat), BF16),
            pltpu.VMEM((slots, BLOCK, BLOCK), BF16),
            pltpu.VMEM((slots, 1, BLOCK), F32),
            pltpu.VMEM((slots, 1, BLOCK), F32),
            pltpu.VMEM((slots, 1, BLOCK), F32),
            pltpu.VMEM((shares, blocks, BLOCK), F32),
            pltpu.VMEM((blocks, BLOCK), F32),
            pltpu.VMEM((shares, width, cols), F32),
            pltpu.VMEM((blocks, width, BLOCK), BF16),
            pltpu.VMEM((slots, width, BLOCK), BF16),
            pltpu.VMEM((slots, width, BLOCK), BF16),
            pltpu.VMEM((slots, width, BLOCK), BF16),
            pltpu.VMEM((slots, width, BLOCK), BF16),
            pltpu.VMEM((slots, width, BLOCK), F32),
            pltpu.VMEM((shares, width, cols), BF16),
            pltpu.VMEM((shares, width, cols), BF16),
            pltpu.VMEM((width // 2, 2 * width), F32),
            pltpu.VMEM((shares, width // 2, 2 * width), F32),
            pltpu.VMEM((width // 2, 2 * width), F32),
            pltpu.VMEM((slots, width // 2, 2 * width), F32),
            dma((5, slots)),
            dma((5, slots)),
            dma((HALVES, slots)),
            dma((HALVES, slots)),
            dma((4, shares)),
            dma((4, shares)),
            dma((3,)),
        ],
        compiler_params=pltpu.CompilerParams(
            collective_id=0, has_side_effects=True, vmem_limit_bytes=60 * 2**20
        ),
        name="subspace",
    )(pair_blocks, pair_live, embeds.reshape(blocks, BLOCK, feat), start)
    return pl.pallas_call(
        functools.partial(basis_kernel, math.sqrt(rows_dev * slots)),
        out_shape=jax.ShapeDtypeStruct((width, cols), F32),
        in_specs=[vmem, vmem],
        out_specs=vmem,
        compiler_params=pltpu.CompilerParams(vmem_limit_bytes=32 * 2**20),
        name="basis",
    )(gram, image)


def solution(mesh):
    placed = (
        P(("groups", "rows"), None),
        P(None, ("groups", "rows", "sub")),
        P(("groups", "rows"), "sub", None, None),
        P(("groups", "rows"), "sub", None),
    )
    return jax.shard_map(
        per_device,
        mesh=mesh,
        in_specs=placed,
        out_specs=P(None, ("groups", "rows", "sub")),
        check_vma=False,
    )
```

time: 80.7 us -> 75.2 us (0.932)
  Pallas kernels: 76.8 us -> 71.9 us
    pallas_call x1, Pallas kernels: 70.3 us -> 65.4 us  [per_device(): pl.pallas_call(functools.partial(subspace_kernel, slots, shares), out_sha...]
    broadcast_in_dim x2 -> x0, local copies, waits for them, and re-layouts: 1.93 us -> none  [per_device(): jnp.broadcast_to(pair_blocks[0, 0, :, 1][:, None, None], (slots, 1, 128))]
    unnamed x4 -> x5, local copies, waits for them, and re-layouts: 1.7 us -> 3 us
where the time goes in v2:
time: 75.2 us; the launch traced here: 74.9 us
  Pallas kernels  71.9 us (96%)
  local copies, waits for them, and re-layouts  3 us (4%)
    pallas_call x1, Pallas kernels, per_device(): pl.pallas_call(functools.partial(subspace_kernel, slots, shares), out_sha...  65.4 us
    pallas_call x1, Pallas kernels, per_device(): pl.pallas_call(functools.partial(basis_kernel, math.sqrt(rows_dev * slots...  6.51 us
    unnamed x5, local copies, waits for them, and re-layouts  3 us

profile of v2, /device:TPU:0, one launch (start us, length us, event | category | flops | bytes accessed | tf_op | source)
XLA Modules:
  0.0 74.9 jit_solution(13018453498152543548)
XLA Ops:
  0.0 1.3 %copy.5.pairs_ref = s32[1,1,4,2]{3,2,1,0:T(4,128)} copy(s32[1,1,4,2]{2,3,1,0:T(2,128)} %param.6) | data formatting | bytes 64 | tf_op args[2]
  1.3 65.4 %subspace.1 = (f32[64,1024]{1,0:T(8,128)}, f32[32,128]{1,0:T(8,128)}) custom-call(s32[1,1,4,2]{3,2,1,0:T(4,128)} %copy.5.pairs_ref, s32[1,1,4]{2,1,0:T(1,128)} %live_ref.1, bf16[8,512,256]{2,1,0:T(8,128)(2,1)} %bitcast.1, f32[64,1024]{1,0:T(8,128)} %start_hbm.1), custom_call_target="tpu_custom_call" | custom-call | tf_op jit(solution)/shard_map/subspace/pallas_call | solution.py:312
  66.7 0.0 copy-start
  66.8 0.9 %copy-done = f32[64,1024]{1,0:T(8,128)S(1)} copy-done((f32[64,1024]{1,0:T(8,128)S(1)}, f32[64,1024]{1,0:T(8,128)}, u32[]{:S(2)}) %copy-start) | copy-done | bytes 262168
  67.7 0.0 copy-start.1
  67.7 0.7 copy-done.1
  68.4 6.5 %basis.1 = f32[64,1024]{1,0:T(8,128)} custom-call(f32[32,128]{1,0:T(8,128)S(1)} %copy-done.1, f32[64,1024]{1,0:T(8,128)S(1)} %copy-done), custom_call_target="tpu_custom_call" | custom-call | tf_op jit(solution)/shard_map/basis/pallas_call | solution.py:360
Async XLA Ops:
  66.7 1.0 %copy-start = (f32[64,1024]{1,0:T(8,128)S(1)}, f32[64,1024]{1,0:T(8,128)}, u32[]{:S(2)}) copy-start(f32[64,1024]{1,0:T(8,128)} %get-tuple-element.8.image_ref) | copy-start | bytes 786436
  67.7 0.7 copy-start.1

commit v3 on v2

--- a/solution.py
+++ b/solution.py
@@ -41,7 +41,7 @@
     slots, shares, pairs_ref, live_ref, embeds_hbm, start_hbm, image_ref, gram_ref,
     embeds, sent_meta, got_meta, served, units, sent_units, got_units, tiles, col_sums, own_sums, got_sums,
     got_degree, degree_out, got_start, scaled, sent_scaled, got_scaled, sent_product, got_product,
-    local_part, sent_products, got_products, gram_out, got_gram_sub, gram_part, got_gram_rows,
+    local_part, local_total, sent_products, got_products, gram_out, got_gram_sub, gram_part, got_gram_rows,
     row_send, row_recv, unit_send, unit_recv, sub_send, sub_recv, local_sem,
 ):
     me_row = lax.axis_index("rows")
@@ -217,21 +217,25 @@
 
     stay(0)
     each(slots, stay, 1)
-    each(slots, lambda d: row_copy(PRODUCT, sent_product.at[other_row(d)], got_product.at[other_row(d)], other_row(d), other_row(d)).wait_recv(), 1)
-
-    def total_of(j):
-        total = jnp.zeros(local_part.shape[1:], F32)
-
-        def add(t, total):
-            there = jnp.where(own(t) == j, 1.0, 0.0)
-            here = jnp.where(partner(t) == j, 1.0, 0.0)
-            return total + here * local_part[t] + there * got_product[t].astype(F32)
-
+
+    def sum_slots(total, add):
         if slots <= 4:
             for t in range(slots):
                 total = add(t, total)
             return total
         return lax.fori_loop(0, slots, add, total)
+
+    def fold_local(j, carry):
+        add = lambda t, total: total + jnp.where(partner(t) == j, 1.0, 0.0) * local_part[t]
+        local_total[j] = sum_slots(jnp.zeros(local_part.shape[1:], F32), add)
+        return carry
+
+    lax.fori_loop(0, blocks, fold_local, 0)
+    each(slots, lambda d: row_copy(PRODUCT, sent_product.at[other_row(d)], got_product.at[other_row(d)], other_row(d), other_row(d)).wait_recv(), 1)
+
+    def total_of(j):
+        add = lambda t, total: total + jnp.where(own(t) == j, 1.0, 0.0) * got_product[t].astype(F32)
+        return sum_slots(local_total[j], add)
 
     def share(d):
         to = other_sub(d)
@@ -338,6 +342,7 @@
             pltpu.VMEM((slots, width, BLOCK), BF16),
             pltpu.VMEM((slots, width, BLOCK), BF16),
             pltpu.VMEM((slots, width, BLOCK), F32),
+            pltpu.VMEM((blocks, width, BLOCK), F32),
             pltpu.VMEM((shares, width, cols), BF16),
             pltpu.VMEM((shares, width, cols), BF16),
             pltpu.VMEM((width // 2, 2 * width), F32),

time: 75.2 us -> 75.2 us (level)
  no operation moved by 1% of the time
where the time goes in v3:
time: 75.2 us; the launch traced here: 74.9 us
  Pallas kernels  71.9 us (96%)
  local copies, waits for them, and re-layouts  3 us (4%)
    pallas_call x1, Pallas kernels, per_device(): pl.pallas_call(functools.partial(subspace_kernel, slots, shares), out_sha...  65.3 us
    pallas_call x1, Pallas kernels, per_device(): pl.pallas_call(functools.partial(basis_kernel, math.sqrt(rows_dev * slots...  6.51 us
    unnamed x5, local copies, waits for them, and re-layouts  3 us

profile of v3, /device:TPU:0, one launch (start us, length us, event | category | flops | bytes accessed | tf_op | source)
XLA Modules:
  0.0 74.9 jit_solution(1473986503677502350)
XLA Ops:
  0.0 1.3 %copy.5.pairs_ref = s32[1,1,4,2]{3,2,1,0:T(4,128)} copy(s32[1,1,4,2]{2,3,1,0:T(2,128)} %param.6) | data formatting | bytes 64 | tf_op args[2]
  1.3 65.3 %subspace.1 = (f32[64,1024]{1,0:T(8,128)}, f32[32,128]{1,0:T(8,128)}) custom-call(s32[1,1,4,2]{3,2,1,0:T(4,128)} %copy.5.pairs_ref, s32[1,1,4]{2,1,0:T(1,128)} %live_ref.1, bf16[8,512,256]{2,1,0:T(8,128)(2,1)} %bitcast.1, f32[64,1024]{1,0:T(8,128)} %start_hbm.1), custom_call_target="tpu_custom_call" | custom-call | tf_op jit(solution)/shard_map/subspace/pallas_call | solution.py:316
  66.7 0.0 copy-start
  66.7 0.9 %copy-done = f32[64,1024]{1,0:T(8,128)S(1)} copy-done((f32[64,1024]{1,0:T(8,128)S(1)}, f32[64,1024]{1,0:T(8,128)}, u32[]{:S(2)}) %copy-start) | copy-done | bytes 262168
  67.6 0.0 copy-start.1
  67.6 0.7 copy-done.1
  68.4 6.5 %basis.1 = f32[64,1024]{1,0:T(8,128)} custom-call(f32[32,128]{1,0:T(8,128)S(1)} %copy-done.1, f32[64,1024]{1,0:T(8,128)S(1)} %copy-done), custom_call_target="tpu_custom_call" | custom-call | tf_op jit(solution)/shard_map/basis/pallas_call | solution.py:365
Async XLA Ops:
  66.7 1.0 %copy-start = (f32[64,1024]{1,0:T(8,128)S(1)}, f32[64,1024]{1,0:T(8,128)}, u32[]{:S(2)}) copy-start(f32[64,1024]{1,0:T(8,128)} %get-tuple-element.8.image_ref) | copy-start | bytes 786436
  67.6 0.7 copy-start.1
